TPU v7x, 1024 devices: a whole 8x8x8 slice. The times are simulated.
1024 devices in a mesh: tok: 4 (over z_hi), fin: 16 (over y, core), fout: 16 (over z_lo, x).
Axes of the slice: x: 8, y: 8, z: 8 (z_hi: 4, z_lo: 2; z = z_hi * 2 + z_lo), core: 2. Of those that a mesh axis runs over, the one named last changes fastest.
Arguments:
- acts: float32 [2048, 12288], P('tok', 'fin'), may hold values from -6 to 6
- weight: float32 [12288, 12288], P(('fin', 'tok'), 'fout'), may hold values from -0.0546875 to 0.0546875
- grad_out: float32 [2048, 12288], P(('tok', 'fin'), 'fout'), may hold values from -6 to 6
Outputs:
- outputs: float32 [2048, 12288], P(('tok', 'fin'), 'fout')
- grad_acts: float32 [2048, 12288], P(('tok', 'fout'), 'fin')
- grad_weight: float32 [12288, 12288], P(('fin', 'tok'), 'fout')
All inputs are finite; a program needn't handle non-finite values.
Results may differ from a plain program's by a relative error of at most 0.000075.
Values sent between devices are 32-bit elements; how exact they have to be, the bound alone decides.
A program may use at most 32 MiB of HBM per device.

v0:
```python
import jax
import jax.numpy as jnp
from jax import lax
from jax.sharding import PartitionSpec as P


def matmul(left, right):
    return jnp.dot(left, right, precision=lax.Precision.HIGHEST, preferred_element_type=jnp.float32)


def matmul_nt(left, right):
    return lax.dot_general(
        left,
        right,
        (((1,), (1,)), ((), ())),
        precision=lax.Precision.HIGHEST,
        preferred_element_type=jnp.float32,
    )


def matmul_tn(left, right):
    return lax.dot_general(
        left,
        right,
        (((0,), (0,)), ((), ())),
        precision=lax.Precision.HIGHEST,
        preferred_element_type=jnp.float32,
    )


def input_gradient(term_rows, rows_here):
    return lax.psum_scatter(
        term_rows(jnp.int32(0), rows_here * lax.axis_size("fout")),
        "fout",
        scatter_dimension=0,
        tiled=True,
    )


def weight_gradient(acts, grads):
    return lax.psum_scatter(matmul_tn(acts, grads), "tok", scatter_dimension=0, tiled=True)


def shards(acts, weight, grad_out):
    fout_rows = acts.shape[0] // lax.axis_size("fout")
    grads = lax.all_gather(grad_out, "fin", axis=0, tiled=True)
    tile = lax.all_gather(weight, "tok", axis=0, tiled=True)

    def input_term(start, count):
        return matmul_nt(grads, tile)

    outputs = lax.psum_scatter(matmul(acts, tile), "fin", scatter_dimension=0, tiled=True)
    grad_acts = input_gradient(input_term, fout_rows)
    grad_weight = weight_gradient(acts, grads)
    return (outputs, grad_acts, grad_weight)


def solution(mesh):
    in_specs = (P("tok", "fin"), P(("fin", "tok"), "fout"), P(("tok", "fin"), "fout"))
    out_specs = (P(("tok", "fin"), "fout"), P(("tok", "fout"), "fin"), P(("fin", "tok"), "fout"))
    return jax.shard_map(shards, mesh=mesh, in_specs=in_specs, out_specs=out_specs, check_vma=False)
```

profile of v0, /device:TPU:1, one launch (start us, length us, event | category | flops | bytes accessed | tf_op | source)
XLA Modules:
  0.0 348.2 jit_solution(1753183371134573918)
XLA Ops:
  7.2 0.0 copy-start
  7.2 0.0 all-gather.3.cloned.1.call-start
  7.2 0.7 all-gather.3.cloned.1.call-update
  7.9 0.0 all-gather.5.cloned.1.call-start
  8.0 0.7 all-gather.5.cloned.1.call-update
  8.7 0.0 reduce-scatter.4.cloned.1.call-start
  8.7 77.1 %all-gather.3.cloned.1.call-done = f32[768,768]{1,0:T(8,128)} async-done(((f32[192,768]{1,0:T(8,128)}), f32[768,768]{1,0:T(8,128)}) %all-gather.3.cloned.1.call-update) | async-done | bytes 2359312 | tf_op jit(solution)/shard_map/all_gather | solution.py:47
  85.8 0.0 copy-done
  85.8 6.8 %fusion = f32[512,768]{1,0:T(8,128)} fusion(f32[512,768]{1,0:T(8,128)S(1)} %copy-done, f32[768,768]{1,0:T(8,128)} %all-gather.3.cloned.1.call-done), kind=kOutput, calls=%fused_computation | convolution fusion | flops 3623878656 | bytes 5505024 | tf_op jit(solution)/shard_map/dot_general | solution.py:8
  92.6 0.0 reduce-scatter.4.cloned.1.call-update
  92.6 0.0 reduce-scatter.6.cloned.1.call-start
  92.7 38.3 %all-gather.5.cloned.1.call-done = f32[512,768]{1,0:T(8,128)} async-done(((f32[32,768]{1,0:T(8,128)}), f32[512,768]{1,0:T(8,128)}) %all-gather.5.cloned.1.call-update) | async-done | bytes 1572880 | tf_op jit(solution)/shard_map/all_gather | solution.py:46
  130.9 7.3 %fusion.1 = f32[512,768]{1,0:T(8,128)} fusion(f32[512,768]{1,0:T(8,128)} %all-gather.5.cloned.1.call-done, f32[768,768]{1,0:T(8,128)} %all-gather.3.cloned.1.call-done), kind=kOutput, calls=%fused_computation.1 | convolution fusion | flops 3623878656 | bytes 5505024 | tf_op jit(solution)/shard_map/dot_general | solution.py:12
  138.2 0.0 copy-start.1
  138.2 0.0 reduce-scatter.6.cloned.1.call-update
  138.3 0.2 reduce-scatter.8.cloned.1.call-start
  138.5 1.2 copy-done.1
  139.7 5.5 %fusion.2 = f32[768,768]{1,0:T(8,128)} fusion(f32[512,768]{1,0:T(8,128)S(1)} %copy-done, f32[512,768]{1,0:T(8,128)S(1)} %copy-done.1), kind=kOutput, calls=%fused_computation.2 | convolution fusion | flops 3623878656 | bytes 5505024 | tf_op jit(solution)/shard_map/dot_general | solution.py:22
  145.2 0.0 reduce-scatter.8.cloned.1.call-update
  145.2 51.9 %reduce-scatter.4.cloned.1.call-done = f32[32,768]{1,0:T(8,128)} async-done(((f32[512,768]{1,0:T(8,128)}), f32[32,768]{1,0:T(8,128)}) %reduce-scatter.4.cloned.1.call-update) | async-done | bytes 98320 | tf_op jit(solution)/shard_map/reduce_scatter | solution.py:52
  197.1 70.8 %reduce-scatter.6.cloned.1.call-done = f32[32,768]{1,0:T(8,128)} async-done(((f32[512,768]{1,0:T(8,128)}), f32[32,768]{1,0:T(8,128)}) %reduce-scatter.6.cloned.1.call-update) | async-done | bytes 98320 | tf_op jit(solution)/shard_map/reduce_scatter | solution.py:32
  267.9 73.7 %reduce-scatter.8.cloned.1.call-done = f32[192,768]{1,0:T(8,128)} async-done(((f32[768,768]{1,0:T(8,128)}), f32[192,768]{1,0:T(8,128)}) %reduce-scatter.8.cloned.1.call-update) | async-done | bytes 589840 | tf_op jit(solution)/shard_map/reduce_scatter | solution.py:41
Async XLA Ops:
  7.2 78.7 %copy-start = (f32[512,768]{1,0:T(8,128)S(1)}, f32[512,768]{1,0:T(8,128)}, u32[]{:S(2)}) copy-start(f32[512,768]{1,0:T(8,128)} %param.3) | copy-start | bytes 4718596
  7.2 78.6 %all-gather.3.cloned.1.call-start = ((), (), s32[]{:S(2)}) async-start(), calls=%async_computation.3 | async-start | bytes 2949120 | tf_op jit(solution)/shard_map/all_gather | solution.py:47
  7.9 123.0 %all-gather.5.cloned.1.call-start = ((), (), s32[]{:S(2)}) async-start(), calls=%async_computation.5 | async-start | bytes 1671168 | tf_op jit(solution)/shard_map/all_gather | solution.py:46
  8.7 188.4 %reduce-scatter.4.cloned.1.call-start = ((), (), s32[]{:S(2)}) async-start(), calls=%async_computation.4 | async-start | bytes 1671168 | tf_op jit(solution)/shard_map/reduce_scatter | solution.py:52
  92.6 175.3 %reduce-scatter.6.cloned.1.call-start = ((), (), s32[]{:S(2)}) async-start(), calls=%async_computation.6 | async-start | bytes 1671168 | tf_op jit(solution)/shard_map/reduce_scatter | solution.py:32
  138.2 1.4 copy-start.1
  138.3 203.3 %reduce-scatter.8.cloned.1.call-start = ((), (), s32[]{:S(2)}) async-start(), calls=%async_computation.7 | async-start | bytes 2949120 | tf_op jit(solution)/shard_map/reduce_scatter | solution.py:41
Sparse Core Ops, SparseCore 0:
  10.7 75.0 all-gather.2
  88.5 42.3 all-gather.4
  134.9 62.1 reduce-scatter.3
  201.3 66.5 reduce-scatter.5
  271.8 69.7 reduce-scatter.7
where the time goes:
time: 348 us
  waiting for transfers between devices  313 us (90%)
  matrix products  19.6 us (6%)
  between operations  13.8 us (4%)
    all_gather x1, waiting for transfers between devices, shards(): tile = lax.all_gather(weight, 'tok', axis=0, tiled=True)  77.1 us
    reduce_scatter x1, waiting for transfers between devices, weight_gradient(): lax.psum_scatter(matmul_tn(acts, grads), 'tok', scatter_dimension=0, tile...  73.7 us
    reduce_scatter x1, waiting for transfers between devices, input_gradient(): lax.psum_scatter(term_rows(jnp.int32(0), rows_here * lax.axis_size('fout'...  70.8 us
    reduce_scatter x1, waiting for transfers between devices, shards(): lax.psum_scatter(matmul(acts, tile), 'fin', scatter_dimension=0, tiled=True)  51.9 us
    all_gather x1, waiting for transfers between devices, shards(): grads = lax.all_gather(grad_out, 'fin', axis=0, tiled=True)  38.3 us
    dot_general x1, matrix products, matmul_nt(): lax.dot_general(left, right, (((1,), (1,)), ((), ())), precision=lax.Prec...  7.31 us
  transfers between devices with their start and end apart: 5, of which 5 were waited for; matrix products, arithmetic and copies ran while one was open for 6% of the time, Pallas kernels for 0%

commit v1 on v0

v1 whole, which is shorter than its diff:
```python
import functools

import jax
import jax.numpy as jnp
from jax import lax
from jax.experimental import pallas as pl
from jax.experimental.pallas import tpu as pltpu
from jax.sharding import PartitionSpec as P

MESH = pl.DeviceIdType.MESH
F32 = jnp.float32


def halves(value):
    high = value.astype(jnp.bfloat16)
    return high, (value - high.astype(F32)).astype(jnp.bfloat16)


def dot3(left, right, left_dim, right_dim):
    dims = (((left_dim,), (right_dim,)), ((), ()))
    dot = functools.partial(lax.dot_general, dimension_numbers=dims, preferred_element_type=F32)
    return dot(left[0], right[0]) + (dot(left[0], right[1]) + dot(left[1], right[0]))


def kernel(sizes, acts, weight, grad, out, grad_acts, grad_weight,
           acts_t, acts_hi, acts_lo, cols, grads, tile, part, part_in, y_up, y_dn, gpart, x_up, x_dn, swap, swap_in,
           send_sem, recv_sem):
    n_tok, n_fin, n_fout = sizes
    n_y, n_x = n_fin // 2, n_fout // 2
    t, i, o = lax.axis_index("tok"), lax.axis_index("fin"), lax.axis_index("fout")
    y, c = i // 2, lax.rem(i, 2)
    zl, x = o // n_x, lax.rem(o, n_x)
    z_up, z_dn, z_op = [(lax.rem(t + d, n_tok), i, o) for d in (1, n_tok - 1, 2)]
    yu, yd = [(t, lax.rem(i + d, n_fin), o) for d in (2, n_fin - 2)]
    core = (t, i + 1 - 2 * c, o)
    xu, xd = [(t, i, zl * n_x + lax.rem(x + d, n_x)) for d in (1, n_x - 1)]
    zlo = (t, i, lax.rem(o + n_x, n_fout))
    rows = grad.shape[0]
    w_rows = weight.shape[0]
    piece = w_rows // n_x
    quarter = w_rows // 4

    barrier = pltpu.get_barrier_semaphore()
    peers = (z_up, z_dn, z_op, yu, yd, core, xu, xd, zlo)
    for peer in peers:
        pl.semaphore_signal(barrier, inc=1, device_id=peer, device_id_type=MESH)
    pl.semaphore_wait(barrier, len(peers))

    started = []

    def copy(src, dst, peer):
        k = len(started)
        cp = pltpu.make_async_remote_copy(src_ref=src, dst_ref=dst, send_sem=send_sem.at[k], recv_sem=recv_sem.at[k],
                                          device_id=peer, device_id_type=MESH)
        cp.start()
        started.append(cp)
        return cp

    events = []

    def at(time, run):
        events.append((time, len(events), run))

    def aligned(start, count):
        return pl.ds(pl.multiple_of(start, 8), count)

    cp = {}

    def zg_start():
        cp["zg_up"] = copy(grad, grads.at[3, aligned(i * rows, rows)], z_up)
        cp["zg_dn"] = copy(grad, grads.at[1, aligned(i * rows, rows)], z_dn)

    def zg_forward():
        h = rows // 2
        first, second = aligned(i * rows, h), aligned(i * rows + h, h)
        cp["zg_up"].wait_recv()
        cp["zg_up2"] = copy(grads.at[3, first], grads.at[2, first], z_up)
        cp["zg_dn"].wait_recv()
        cp["zg_dn2"] = copy(grads.at[1, second], grads.at[2, second], z_dn)

    def zg_end():
        cp["zg_up2"].wait_recv()
        cp["zg_dn2"].wait_recv()

    def ring_start(key, piece_of, m, n, up, dn):
        cp[key, "up", 1] = copy(piece_of(m, 0), piece_of(m, 0), up)
        cp[key, "dn", 1] = copy(piece_of(m, 0), piece_of(m, 0), dn)

    def ring_step(key, step, piece_of, m, n, up, dn, arrived):
        last = n // 2
        lo, hi = lax.rem(m + n - step, n), lax.rem(m + step, n)
        nxt = step + 1
        cp[key, "up", step].wait_recv()
        if nxt <= last:
            part_no = 1 if nxt == last else 0
            cp[key, "up", nxt] = copy(piece_of(lo, part_no), piece_of(lo, part_no), up)
            if arrived:
                arrived(lo)
        cp[key, "dn", step].wait_recv()
        if nxt <= last:
            part_no = 2 if nxt == last else 0
            cp[key, "dn", nxt] = copy(piece_of(hi, part_no), piece_of(hi, part_no), dn)
            if arrived:
                arrived(hi)
        elif arrived:
            arrived(lo)

    def grad_rows(first, count, core_no):
        def piece_of(m, part_no):
            base = (2 * m + core_no) * rows
            h = rows // 2
            span = (aligned(base, rows), aligned(base, h), aligned(base + h, h))[part_no]
            return grads.at[pl.ds(first, count), span]
        return piece_of

    def core_copies(key, first, count):
        def arrived(m):
            ref = grad_rows(first, count, c)(m, 0)
            cp.setdefault((key, "core"), []).append(copy(ref, ref, core))
        return arrived

    ya = grad_rows(0, 1, c), y, n_y, yu, yd
    yb = grad_rows(1, n_tok - 1, c), y, n_y, yu, yd
    ya_core, yb_core = core_copies("ya", 0, 1), core_copies("yb", 1, n_tok - 1)

    def ya_start():
        grads[0, aligned(i * rows, rows), :] = grad[...]
        ring_start("ya", *ya)
        ya_core(y)

    def yb_start():
        ring_start("yb", *yb)
        yb_core(y)

    def cols_of(m, part_no):
        cut = 16
        span = (aligned(m * piece, piece), aligned(m * piece, cut), aligned(m * piece + cut, piece - cut))[part_no]
        return cols.at[pl.ds(1, n_tok - 1), span]

    xa = cols_of, x, n_x, xu, xd

    def acts_start():
        acts_t[...] = acts[...].T
        for d, peer in ((1, z_up), (3, z_dn), (2, z_op)):
            span = aligned(lax.rem(t + d, n_tok) * w_rows + x * piece, piece)
            cp["a2a", d] = copy(acts_t.at[span], cols.at[n_tok - d, aligned(x * piece, piece)], peer)

    def acts_split():
        acts_hi[...], acts_lo[...] = halves(acts_t[...])

    def xa_start():
        for d in (1, 3, 2):
            cp["a2a", d].wait_recv()
        ring_start("xa", *xa)

    def w_span(k):
        return pl.ds(k * quarter, quarter)

    def w_start():
        for ku, kd in ((0, 2), (1, 3), (2, 0), (3, 1)):
            cp["w_up", ku] = copy(weight.at[w_span(ku)], tile.at[t, w_span(ku)], z_up)
            cp["w_dn", kd] = copy(weight.at[w_span(kd)], tile.at[t, w_span(kd)], z_dn)
        tile[t] = weight[...]

    before, after, across = [lax.rem(t + d, n_tok) for d in (n_tok - 1, 1, 2)]

    def w_forward(k):
        cp["w_up", k].wait_recv()
        cp["w_up2", k] = copy(tile.at[before, w_span(k)], tile.at[before, w_span(k)], z_up)
        cp["w_dn", k + 2].wait_recv()
        cp["w_dn2", k + 2] = copy(tile.at[after, w_span(k + 2)], tile.at[after, w_span(k + 2)], z_dn)

    def w_near():
        for k in (2, 3):
            cp["w_up", k].wait_recv()
            cp["w_dn", k - 2].wait_recv()

    def w_far():
        for k in (0, 1):
            cp["w_up2", k].wait_recv()
            cp["w_dn2", k + 2].wait_recv()

    def out_term(block):
        span = pl.ds(pl.multiple_of(block * w_rows, 16), w_rows)
        return dot3((acts_hi[span], acts_lo[span]), halves(tile[block]), 0, 0)

    def out_store(value, add):
        for m in range(n_y):
            for k in range(2):
                rows_of = value[(2 * m + k) * rows:(2 * m + k + 1) * rows]
                part[k, m] = part[k, m] + rows_of if add else rows_of

    def out_near():
        out_store(out_term(t), False)
        out_store(out_term(before), True)
        out_store(out_term(after), True)

    def out_far():
        out_store(out_term(across), True)
        cp["pair"] = copy(part.at[1 - c], part_in, core)

    def scatter_start(key, dest, m, n, up, dn, slots):
        mid = lax.rem(m + n // 2, n)
        cp[key, "up", 0] = copy(dest(mid, 1), slots(0, 0, 1), up)
        cp[key, "dn", 0] = copy(dest(mid, 2), slots(1, 0, 2), dn)

    def scatter_step(key, step, dest, m, n, up, dn, slots):
        for way, peer in ((0, up), (1, dn)):
            name = ("up", "dn")[way]
            gap = n // 2 - step
            to = lax.rem(m + (gap if way == 0 else n - gap), n)
            part_no = (1 + way) if step == 1 else 0
            cp[key, name, step - 1].wait_recv()
            ref = dest(to, part_no)
            ref[...] = ref[...] + slots(way, step - 1, part_no)[...]
            cp[key, name, step] = copy(dest(to, 0), slots(way, step, 0), peer)

    def scatter_end(key, dest, m, n, up, dn, slots):
        last = n // 2 - 1
        cp[key, "up", last].wait_recv()
        cp[key, "dn", last].wait_recv()
        return dest(m, 0)[...] + slots(0, last, 0)[...] + slots(1, last, 0)[...]

    def out_dest(m, part_no):
        h = rows // 2
        return part.at[c, m, (pl.ds(0, rows), pl.ds(0, h), pl.ds(h, h))[part_no]]

    def out_slots(way, step, part_no):
        h = rows // 2
        return (y_up, y_dn)[way].at[step, (pl.ds(0, rows), pl.ds(0, h), pl.ds(h, h))[part_no]]

    yr = out_dest, y, n_y, yu, yd, out_slots

    def out_pair():
        cp["pair"].wait_recv()
        part[c] = part[c] + part_in[...]
        scatter_start("yr", *yr)

    def out_end():
        out[...] = scatter_end("yr", *yr)

    pair = t // 2

    def ga_of(k):
        def dest(m, part_no):
            return gpart.at[k, m, (pl.ds(0, 2), pl.ds(0, 1), pl.ds(1, 1))[part_no]]

        def slots(way, step, part_no):
            return (x_up, x_dn)[way].at[k, step, (pl.ds(0, 2), pl.ds(0, 1), pl.ds(1, 1))[part_no]]

        return dest, x, n_x, xu, xd, slots

    def ga_start(k):
        which = pair if k == 0 else 1 - pair
        blocks = tile[pl.ds(2 * which, 2)].reshape(2 * w_rows, weight.shape[1])
        value = dot3(halves(grads[0]), halves(blocks), 1, 1)
        for m in range(n_x):
            for z in range(2):
                gpart[k, m, z] = value[(z * n_x + m) * rows:(z * n_x + m + 1) * rows]
        scatter_start(("xr", k), *ga_of(k))

    def ga_swap(k):
        swap[k] = scatter_end(("xr", k), *ga_of(k))
        cp["zlo", k] = copy(swap.at[k, 1 - zl], swap_in.at[k], zlo)

    def ga_end():
        value = []
        for k in range(2):
            cp["zlo", k].wait_recv()
            value.append(swap[k, zl] + swap_in[k])
        width = value[0].shape[1]
        grad_acts[:, :width] = jnp.where(pair == 0, value[0], value[1])
        grad_acts[:, width:] = jnp.where(pair == 0, value[1], value[0])

    def wait_core(key):
        for copied in cp[key, "core"]:
            copied.wait_recv()

    def gw():
        own = pl.ds(pl.multiple_of(t * w_rows, 16), w_rows)
        total = dot3((acts_hi[own], acts_lo[own]), halves(grads[0]), 1, 0)
        for d in range(1, n_tok):
            total = total + dot3(halves(cols[d]), halves(grads[d]), 1, 0)
        grad_weight[...] = total

    at(0, zg_start)
    at(0.1, ya_start)
    at(0.2, acts_start)
    at(0.3, w_start)
    at(0.4, acts_split)
    at(4, zg_forward)
    at(5, lambda: ring_step("ya", 1, *ya, ya_core))
    at(7, xa_start)
    at(8, zg_end)
    at(8.1, yb_start)
    at(9, lambda: ring_step("ya", 2, *ya, ya_core))
    at(12, lambda: w_forward(0))
    at(13, lambda: ring_step("xa", 1, *xa, None))
    at(14, lambda: ring_step("ya", 3, *ya, ya_core))
    at(18, lambda: ring_step("ya", 4, *ya, ya_core))
    at(18.5, lambda: ring_step("xa", 2, *xa, None))
    at(19, lambda: w_forward(1))
    at(19.5, lambda: ring_step("yb", 1, *yb, yb_core))
    at(23, lambda: ring_step("xa", 3, *xa, None))
    at(26, lambda: ring_step("yb", 2, *yb, yb_core))
    at(26.5, lambda: ring_step("xa", 4, *xa, None))
    at(27, w_near)
    at(27.1, lambda: wait_core("ya"))
    at(27.2, lambda: ga_start(0))
    at(27.5, out_near)
    at(32, lambda: scatter_step(("xr", 0), 1, *ga_of(0)))
    at(34, lambda: ring_step("yb", 3, *yb, yb_core))
    at(36, lambda: scatter_step(("xr", 0), 2, *ga_of(0)))
    at(40, lambda: scatter_step(("xr", 0), 3, *ga_of(0)))
    at(41, lambda: ring_step("yb", 4, *yb, yb_core))
    at(44, lambda: ga_swap(0))
    at(45, w_far)
    at(45.1, out_far)
    at(45.2, lambda: ga_start(1))
    at(46, out_pair)
    at(46.5, lambda: wait_core("yb"))
    at(46.6, gw)
    for s in (1, 2, 3):
        at(46 + 4 * s, lambda s=s: scatter_step("yr", s, *yr))
        at(46.1 + 4 * s, lambda s=s: scatter_step(("xr", 1), s, *ga_of(1)))
    at(62, lambda: ga_swap(1))
    at(63, out_end)
    at(66, ga_end)
    for _, _, run in sorted(events, key=lambda event: event[:2]):
        run()
    for cp_started in started:
        cp_started.wait_send()


def shards(sizes, acts, weight, grad_out):
    n_tok, n_fin, n_fout = sizes
    n_y, n_x = n_fin // 2, n_fout // 2
    toks, depth = acts.shape
    w_rows, width = weight.shape
    rows = grad_out.shape[0]
    half = depth // 2
    vmem = pl.BlockSpec(memory_space=pltpu.VMEM)
    return pl.pallas_call(
        functools.partial(kernel, sizes),
        out_shape=(
            jax.ShapeDtypeStruct((rows, width), F32),
            jax.ShapeDtypeStruct((rows, depth), F32),
            jax.ShapeDtypeStruct((w_rows, width), F32),
        ),
        in_specs=[vmem] * 3,
        out_specs=(vmem,) * 3,
        scratch_shapes=[
            pltpu.VMEM((depth, toks), F32),
            pltpu.VMEM((depth, toks), jnp.bfloat16),
            pltpu.VMEM((depth, toks), jnp.bfloat16),
            pltpu.VMEM((n_tok, w_rows, toks), F32),
            pltpu.VMEM((n_tok, toks, width), F32),
            pltpu.VMEM((n_tok, w_rows, width), F32),
            pltpu.VMEM((2, n_y, rows, width), F32),
            pltpu.VMEM((n_y, rows, width), F32),
            pltpu.VMEM((n_y // 2, rows, width), F32),
            pltpu.VMEM((n_y // 2, rows, width), F32),
            pltpu.VMEM((2, n_x, 2, rows, half), F32),
            pltpu.VMEM((2, n_x // 2, 2, rows, half), F32),
            pltpu.VMEM((2, n_x // 2, 2, rows, half), F32),
            pltpu.VMEM((2, 2, rows, half), F32),
            pltpu.VMEM((2, rows, half), F32),
            pltpu.SemaphoreType.DMA((96,)),
            pltpu.SemaphoreType.DMA((96,)),
        ],
        compiler_params=pltpu.CompilerParams(collective_id=0, has_side_effects=True, vmem_limit_bytes=52 * 2**20),
    )(acts, weight, grad_out)


def solution(mesh):
    sizes = tuple(mesh.shape[name] for name in ("tok", "fin", "fout"))
    in_specs = (P("tok", "fin"), P(("fin", "tok"), "fout"), P(("tok", "fin"), "fout"))
    out_specs = (P(("tok", "fin"), "fout"), P(("tok", "fout"), "fin"), P(("fin", "tok"), "fout"))
    return jax.shard_map(functools.partial(shards, sizes), mesh=mesh, in_specs=in_specs, out_specs=out_specs, check_vma=False)
```

time: 348 us -> 132 us (0.38)
  waiting for transfers between devices: 313 us -> 0 us
  Pallas kernels: 0 us -> 124 us
  matrix products: 19.6 us -> 0 us
  between operations: 13.8 us -> 0.65 us
    reduce_scatter x3 -> x0, waiting for transfers between devices: 196 us -> none  [the longest x1 73.7 us: weight_gradient(): lax.psum_scatter(matmul_tn(acts, grads), 'tok', scatter_dimension=0, tile...]
    pallas_call x0 -> x1, Pallas kernels: none -> 124 us  [shards(): pl.pallas_call(functools.partial(kernel, sizes), out_shape=(jax.ShapeDtyp...]
    all_gather x2 -> x0, waiting for transfers between devices: 115 us -> none  [the longest x1 77.1 us: shards(): tile = lax.all_gather(weight, 'tok', axis=0, tiled=True)]
    dot_general x3 -> x0, matrix products: 19.6 us -> none  [the longest x1 7.31 us: matmul_nt(): lax.dot_general(left, right, (((1,), (1,)), ((), ())), precision=lax.Prec...]
  transfers between devices with their start and end apart: 5 -> 0, of which waited for: 5 -> 0; matrix products, arithmetic and copies ran while one was open for 6% -> 0% of each run, Pallas kernels for 0% -> 0%
where the time goes in v1:
time: 132 us; the launch traced here: 129 us
  Pallas kernels  124 us (94%)
  local copies, waits for them, and re-layouts  4.05 us (3%)
    pallas_call x1, Pallas kernels, shards(): pl.pallas_call(functools.partial(kernel, sizes), out_shape=(jax.ShapeDtyp...  124 us
    unnamed x7, local copies, waits for them, and re-layouts  4.05 us

profile of v1, /device:TPU:1, one launch (start us, length us, event | category | flops | bytes accessed | tf_op | source)
XLA Modules:
  0.0 129.2 jit_solution(15997233436190375464)
XLA Ops:
  0.6 0.0 copy-start
  0.6 1.1 copy-done
  1.7 0.0 copy-start.1
  1.7 0.9 copy-done.1
  2.6 124.5 %shard_map.58 = (f32[32,768]{1,0:T(8,128)S(1)}, f32[32,768]{1,0:T(8,128)S(1)}, f32[192,768]{1,0:T(8,128)S(1)}) custom-call(f32[512,768]{1,0:T(8,128)} %acts.1, f32[192,768]{1,0:T(8,128)S(1)} %copy-done, f32[32,768]{1,0:T(8,128)S(1)} %copy-done.1), custom_call_target="tpu_custom_call" | custom-call | tf_op jit(solution)/shard_map/pallas_call | solution.py:343
  127.1 0.6 copy.9
  127.7 0.6 copy.10
  128.3 0.8 copy.11
Async XLA Ops:
  0.6 1.1 copy-start
  1.7 0.9 copy-start.1

commit v2 on v0

v2 whole, which is shorter than its diff:
```python
import functools

import jax
import jax.numpy as jnp
from jax import lax
from jax.experimental import pallas as pl
from jax.experimental.pallas import tpu as pltpu
from jax.sharding import PartitionSpec as P

MESH = pl.DeviceIdType.MESH
F32 = jnp.float32

ORDER = (
    "zg0", "ya0", "a0", "w01", "w00", "yad1", "yad2", "zfd", "zfu", "w03", "yb0", "w02", "yau1", "xa0", "wfu1",
    "xad1", "yau2", "ybd1", "as", "yad3", "wfd1", "yc0", "xau1", "yau3", "ybu1", "ya4", "xau2", "yaw", "wfu0",
    "ybu2", "xad2", "wfd0", "ybd2", "wn", "xau3", "ycu1", "x00", "x0u1", "ycu2", "x0d1", "ycd1", "ybd3", "wfar",
    "pair", "g1", "x100", "ybu3", "x0d2", "ycu3", "yr00", "ycd2", "x10u1", "x10d1", "yb4", "x0u2", "yr0d1", "xad3",
    "yr0u1", "x10u2", "x10d2", "ycd3", "x0u3", "x0d3", "yr0d2", "yr0u2", "x10u3", "x10d3", "yc4", "ycw", "ybw",
    "yr0d3", "yr0u3", "xa4", "x04", "x104", "gw", "yr04", "end",
)


def halves(value):
    high = value.astype(jnp.bfloat16)
    return high, (value - high.astype(F32)).astype(jnp.bfloat16)


def dot3(left, right, left_dim, right_dim):
    dims = (((left_dim,), (right_dim,)), ((), ()))
    dot = functools.partial(lax.dot_general, dimension_numbers=dims, preferred_element_type=F32)
    return dot(left[0], right[0]) + (dot(left[0], right[1]) + dot(left[1], right[0]))


def kernel(sizes, acts_in, weight_in, grad_in, out, grad_acts, grad_weight,
           acts, acts_t, acts_hi, acts_lo, cols, grads, tile, part, part_in, y_up, y_dn, gpart, x_up, x_dn, swap, swap_in,
           send_sem, recv_sem, local_sem):
    n_tok, n_fin, n_fout = sizes
    n_y, n_x = n_fin // 2, n_fout // 2
    t, i, o = lax.axis_index("tok"), lax.axis_index("fin"), lax.axis_index("fout")
    y, c = i // 2, lax.rem(i, 2)
    zl, x = o // n_x, lax.rem(o, n_x)
    z_up, z_dn = [(lax.rem(t + d, n_tok), i, o) for d in (1, n_tok - 1)]
    yu, yd = [(t, lax.rem(i + d, n_fin), o) for d in (2, n_fin - 2)]
    core = (t, i + 1 - 2 * c, o)
    xu, xd = [(t, i, zl * n_x + lax.rem(x + d, n_x)) for d in (1, n_x - 1)]
    zlo = (t, i, lax.rem(o + n_x, n_fout))
    z_op = (lax.rem(t + 2, n_tok), i, lax.rem(o + n_x, n_fout))
    rows, w_rows = grad_in.shape[0], weight_in.shape[0]
    piece = w_rows // n_x
    quarter = w_rows // 4

    def aligned(start, count):
        return pl.ds(pl.multiple_of(start, 8), count)

    mine = aligned(i * rows, rows)
    loads = [
        pltpu.make_async_copy(grad_in, grads.at[0, mine], local_sem.at[0]),
        pltpu.make_async_copy(weight_in, tile.at[t], local_sem.at[1]),
        pltpu.make_async_copy(acts_in, acts, local_sem.at[2]),
    ]
    for load in loads:
        load.start()

    barrier = pltpu.get_barrier_semaphore()
    peers = (z_up, z_dn, z_op, yu, yd, core, xu, xd, zlo)
    for peer in peers:
        pl.semaphore_signal(barrier, inc=1, device_id=peer, device_id_type=MESH)
    pl.semaphore_wait(barrier, len(peers))
    for load in loads:
        load.wait()

    started = []
    cp = {}
    events = {}

    def copy(key, src, dst, peer):
        k = len(started)
        cp[key] = pltpu.make_async_remote_copy(src_ref=src, dst_ref=dst, send_sem=send_sem.at[k], recv_sem=recv_sem.at[k],
                                               device_id=peer, device_id_type=MESH)
        cp[key].start()
        started.append(cp[key])

    waited = set()

    def got(*keys):
        for key in keys:
            if key not in waited:
                waited.add(key)
                cp[key].wait_recv()

    def event(name):
        def add(run):
            events[name] = run
            return run
        return add


    h = rows // 2
    first, second = aligned(i * rows, h), aligned(i * rows + h, h)

    @event("zg0")
    def _():
        copy("zgu", grads.at[0, mine], grads.at[2, mine], z_up)
        copy("zgd", grads.at[0, mine], grads.at[1, mine], z_dn)

    @event("zfu")
    def _():
        got("zgu")
        copy("zgu2", grads.at[2, first], grads.at[3, first], z_up)

    @event("zfd")
    def _():
        got("zgd")
        copy("zgd2", grads.at[1, second], grads.at[3, second], z_dn)

    def gather(key, piece_of, m, n, up, dn, to_core, need):
        last = n // 2

        def begin():
            got(*need)
            copy(key + "u1", piece_of(m, 0), piece_of(m, 0), up)
            copy(key + "d1", piece_of(m, 0), piece_of(m, 0), dn)
            if to_core:
                copy(key + "c", piece_of(m, 0), piece_of(m, 0), core)

        def step(way, s):
            back = lax.rem(m + (n - s if way == "u" else s), n)
            got(f"{key}{way}{s}")
            k = 0 if s + 1 < last else (1 if way == "u" else 2)
            copy(f"{key}{way}{s + 1}", piece_of(back, k), piece_of(back, k), up if way == "u" else dn)
            if to_core:
                copy(f"{key}c{way}{s}", piece_of(back, 0), piece_of(back, 0), core)

        def finish():
            got(f"{key}u{last}", f"{key}d{last}")
            if to_core:
                back = lax.rem(m + last, n)
                copy(f"{key}c{last}", piece_of(back, 0), piece_of(back, 0), core)

        events[key + "0"] = begin
        for s in range(1, last):
            for way in "ud":
                events[f"{key}{way}{s}"] = functools.partial(step, way, s)
        events[f"{key}{last}"] = finish
        if to_core:
            inner = [f"{key}c{way}{s}" for s in range(1, last) for way in "ud"]
            events[key + "w"] = lambda: got(key + "c", *inner, f"{key}c{last}")

    def grad_rows(slots):
        def piece_of(m, k):
            base = (2 * m + c) * rows
            return grads.at[slots, (aligned(base, rows), aligned(base, h), aligned(base + h, h))[k]]
        return piece_of

    gather("ya", grad_rows(pl.ds(0, 1)), y, n_y, yu, yd, True, ())
    gather("yb", grad_rows(pl.ds(1, 2)), y, n_y, yu, yd, True, ())
    gather("yc", grad_rows(pl.ds(3, 1)), y, n_y, yu, yd, True, ("zgu2", "zgd2"))

    def cols_of(m, k):
        cut = 16
        base = m * piece
        return cols.at[pl.ds(1, n_tok - 1), (aligned(base, piece), aligned(base, cut), aligned(base + cut, piece - cut))[k]]

    gather("xa", cols_of, x, n_x, xu, xd, False, ("a1", "a3", "a2"))

    @event("a0")
    def _():
        acts_t[...] = acts[...].T
        for d, slot, peer in ((1, 2, z_up), (3, 1, z_dn), (2, 3, z_op)):
            span = aligned(lax.rem(t + d, n_tok) * w_rows + x * piece, piece)
            copy(f"a{d}", acts_t.at[span], cols.at[slot, aligned(x * piece, piece)], peer)

    @event("as")
    def _():
        acts_hi[...], acts_lo[...] = halves(acts_t[...])

    before, after, across = [lax.rem(t + d, n_tok) for d in (n_tok - 1, 1, 2)]

    def w_part(block, k):
        return tile.at[block, pl.ds(k * quarter, quarter)]

    def w_first(k):
        other = (k + 2) % 4
        copy(f"wu{k}", w_part(t, k), w_part(t, k), z_up)
        copy(f"wd{k}", w_part(t, other), w_part(t, other), z_dn)

    def w_up(k):
        got(f"wu{k}")
        copy(f"vu{k}", w_part(before, k), w_part(before, k), z_up)

    def w_dn(k):
        got(f"wd{k}")
        copy(f"vd{k}", w_part(after, k + 2), w_part(after, k + 2), z_dn)

    for k in range(4):
        events[f"w0{k}"] = functools.partial(w_first, k)
    for k in range(2):
        events[f"wfu{k}"] = functools.partial(w_up, k)
        events[f"wfd{k}"] = functools.partial(w_dn, k)

    def out_add(blocks, add):
        value = None
        for block in blocks:
            span = pl.ds(pl.multiple_of(block * w_rows, 16), w_rows)
            term = dot3((acts_hi[span], acts_lo[span]), halves(tile[block]), 0, 0)
            value = term if value is None else value + term
        for m in range(n_y):
            for k in range(2):
                rows_of = value[(2 * m + k) * rows:(2 * m + k + 1) * rows]
                part[k, m] = part[k, m] + rows_of if add else rows_of

    @event("wn")
    def _():
        got(*[f"w{way}{k}" for way in "ud" for k in range(4)])
        out_add((t, before, after), False)

    @event("wfar")
    def _():
        got("vu0", "vu1", "vd0", "vd1")
        out_add((across,), True)

    @event("pair")
    def _():
        copy("pair", part.at[1 - c], part_in, core)

    def scatter(key, dest, slots, m, n, up, dn, ready, done):
        last = n // 2 - 1

        def begin():
            ready()
            mid = lax.rem(m + n // 2, n)
            copy(key + "u0", dest(mid, 1), slots(0, 0, 1), up)
            copy(key + "d0", dest(mid, 2), slots(1, 0, 2), dn)

        def step(way, s):
            gap = n // 2 - s
            to = lax.rem(m + (n - gap if way else gap), n)
            k = 1 + way if s == 1 else 0
            name = "ud"[way]
            got(f"{key}{name}{s - 1}")
            dest(to, k)[...] = dest(to, k)[...] + slots(way, s - 1, k)[...]
            copy(f"{key}{name}{s}", dest(to, 0), slots(way, s, 0), dn if way else up)

        def finish():
            got(f"{key}u{last}", f"{key}d{last}")
            done(dest(m, 0)[...] + slots(0, last, 0)[...] + slots(1, last, 0)[...])

        events[key + "0"] = begin
        for s in range(1, last + 1):
            for way in range(2):
                events[f"{key}{'ud'[way]}{s}"] = functools.partial(step, way, s)
        events[f"{key}{last + 1}"] = finish

    row_parts = (pl.ds(0, rows), pl.ds(0, h), pl.ds(h, h))

    def out_ready():
        got("pair")
        part[c] = part[c] + part_in[...]

    def out_done(value):
        out[...] = value

    scatter("yr0", lambda m, k: part.at[c, m, row_parts[k]], lambda way, s, k: (y_up, y_dn)[way].at[s, row_parts[k]],
            y, n_y, yu, yd, out_ready, out_done)

    pair = t // 2
    zlo_parts = (pl.ds(0, 2), pl.ds(0, 1), pl.ds(1, 1))

    def ga_compute(k):
        which = 1 - pair if k else pair
        blocks = tile[pl.ds(2 * which, 2)].reshape(2 * w_rows, weight_in.shape[1])
        value = dot3(halves(grads[0]), halves(blocks), 1, 1)
        for m in range(n_x):
            for z in range(2):
                gpart[k, m, z] = value[(z * n_x + m) * rows:(z * n_x + m + 1) * rows]

    def ga_scatter(key, k, ready):
        def done(value):
            swap[k] = value
            copy(f"l{k}", swap.at[k, 1 - zl], swap_in.at[k], zlo)

        scatter(key, lambda m, j: gpart.at[k, m, zlo_parts[j]], lambda way, s, j: (x_up, x_dn)[way].at[k, s, zlo_parts[j]],
                x, n_x, xu, xd, ready, done)

    ga_scatter("x0", 0, functools.partial(ga_compute, 0))
    events["g1"] = functools.partial(ga_compute, 1)
    ga_scatter("x10", 1, lambda: None)

    @event("gw")
    def _():
        own = pl.ds(pl.multiple_of(t * w_rows, 16), w_rows)
        total = dot3((acts_hi[own], acts_lo[own]), halves(grads[0]), 1, 0)
        for slot in range(1, n_tok):
            total = total + dot3(halves(cols[slot]), halves(grads[slot]), 1, 0)
        grad_weight[...] = total

    @event("end")
    def _():
        got("l0", "l1")
        value = [swap[k, zl] + swap_in[k] for k in range(2)]
        width = value[0].shape[1]
        grad_acts[:, :width] = jnp.where(pair == 0, value[0], value[1])
        grad_acts[:, width:] = jnp.where(pair == 0, value[1], value[0])

    for name in ORDER:
        events.pop(name)()
    assert not events
    for sent in started:
        sent.wait_send()


def shards(sizes, acts, weight, grad_out):
    n_tok, n_fin, n_fout = sizes
    n_y, n_x = n_fin // 2, n_fout // 2
    toks, depth = acts.shape
    w_rows, width = weight.shape
    rows = grad_out.shape[0]
    half = depth // 2
    vmem = pl.BlockSpec(memory_space=pltpu.VMEM)
    return pl.pallas_call(
        functools.partial(kernel, sizes),
        out_shape=(
            jax.ShapeDtypeStruct((rows, width), F32),
            jax.ShapeDtypeStruct((rows, depth), F32),
            jax.ShapeDtypeStruct((w_rows, width), F32),
        ),
        in_specs=[pl.BlockSpec(memory_space=pl.ANY)] * 3,
        out_specs=(vmem,) * 3,
        scratch_shapes=[
            pltpu.VMEM((toks, depth), F32),
            pltpu.VMEM((depth, toks), F32),
            pltpu.VMEM((depth, toks), jnp.bfloat16),
            pltpu.VMEM((depth, toks), jnp.bfloat16),
            pltpu.VMEM((n_tok, w_rows, toks), F32),
            pltpu.VMEM((n_tok, toks, width), F32),
            pltpu.VMEM((n_tok, w_rows, width), F32),
            pltpu.VMEM((2, n_y, rows, width), F32),
            pltpu.VMEM((n_y, rows, width), F32),
            pltpu.VMEM((n_y // 2, rows, width), F32),
            pltpu.VMEM((n_y // 2, rows, width), F32),
            pltpu.VMEM((2, n_x, 2, rows, half), F32),
            pltpu.VMEM((2, n_x // 2, 2, rows, half), F32),
            pltpu.VMEM((2, n_x // 2, 2, rows, half), F32),
            pltpu.VMEM((2, 2, rows, half), F32),
            pltpu.VMEM((2, rows, half), F32),
            pltpu.SemaphoreType.DMA((112,)),
            pltpu.SemaphoreType.DMA((112,)),
            pltpu.SemaphoreType.DMA((3,)),
        ],
        compiler_params=pltpu.CompilerParams(collective_id=0, has_side_effects=True, vmem_limit_bytes=54 * 2**20),
    )(acts, weight, grad_out)


def solution(mesh):
    sizes = tuple(mesh.shape[name] for name in ("tok", "fin", "fout"))
    in_specs = (P("tok", "fin"), P(("fin", "tok"), "fout"), P(("tok", "fin"), "fout"))
    out_specs = (P(("tok", "fin"), "fout"), P(("tok", "fout"), "fin"), P(("fin", "tok"), "fout"))
    return jax.shard_map(functools.partial(shards, sizes), mesh=mesh, in_specs=in_specs, out_specs=out_specs, check_vma=False)
```

time: 348 us -> 106 us (0.30)
  waiting for transfers between devices: 313 us -> 0 us
  Pallas kernels: 0 us -> 100 us
  matrix products: 19.6 us -> 0 us
  between operations: 13.8 us -> 0.64 us
  local copies, waits for them, and re-layouts: 1.16 us -> 4.99 us
    reduce_scatter x3 -> x0, waiting for transfers between devices: 196 us -> none  [the longest x1 73.7 us: weight_gradient(): lax.psum_scatter(matmul_tn(acts, grads), 'tok', scatter_dimension=0, tile...]
    all_gather x2 -> x0, waiting for transfers between devices: 115 us -> none  [the longest x1 77.1 us: shards(): tile = lax.all_gather(weight, 'tok', axis=0, tiled=True)]
    pallas_call x0 -> x1, Pallas kernels: none -> 100 us  [shards(): pl.pallas_call(functools.partial(kernel, sizes), out_shape=(jax.ShapeDtyp...]
    dot_general x3 -> x0, matrix products: 19.6 us -> none  [the longest x1 7.31 us: matmul_nt(): lax.dot_general(left, right, (((1,), (1,)), ((), ())), precision=lax.Prec...]
    unnamed x4 -> x3, local copies, waits for them, and re-layouts: 1.16 us -> 4.99 us
  transfers between devices with their start and end apart: 5 -> 0, of which waited for: 5 -> 0; matrix products, arithmetic and copies ran while one was open for 6% -> 0% of each run, Pallas kernels for 0% -> 0%
where the time goes in v2:
time: 106 us
  Pallas kernels  100 us (94%)
  local copies, waits for them, and re-layouts  4.99 us (5%)
    pallas_call x1, Pallas kernels, shards(): pl.pallas_call(functools.partial(kernel, sizes), out_shape=(jax.ShapeDtyp...  100 us
    unnamed x3, local copies, waits for them, and re-layouts  4.99 us

profile of v2, /device:TPU:1, one launch (start us, length us, event | category | flops | bytes accessed | tf_op | source)
XLA Modules:
  0.0 105.7 jit_solution(17817360122476312109)
XLA Ops:
  0.6 100.0 %shard_map.58 = (f32[32,768]{1,0:T(8,128)}, f32[32,768]{1,0:T(8,128)}, f32[192,768]{1,0:T(8,128)}) custom-call(f32[512,768]{1,0:T(8,128)} %acts_in.1, f32[192,768]{1,0:T(8,128)} %weight_in.1, f32[32,768]{1,0:T(8,128)} %grad_in.1), custom_call_target="tpu_custom_call" | custom-call | tf_op jit(solution)/shard_map/pallas_call | solution.py:320
  100.7 1.5 %copy.9 = f32[32,768]{1,0:T(8,128)} copy(f32[32,768]{1,0:T(8,128)} %get-tuple-element.6) | data formatting | bytes 196608
  102.2 1.5 %copy.10 = f32[32,768]{1,0:T(8,128)} copy(f32[32,768]{1,0:T(8,128)} %get-tuple-element.7) | data formatting | bytes 196608
  103.8 1.9 %copy.11 = f32[192,768]{1,0:T(8,128)} copy(f32[192,768]{1,0:T(8,128)} %get-tuple-element.8) | data formatting | bytes 1179648

commit v3 on v2

--- a/solution.py
+++ b/solution.py
@@ -11,12 +11,13 @@
 F32 = jnp.float32
 
 ORDER = (
-    "zg0", "ya0", "a0", "w01", "w00", "yad1", "yad2", "zfd", "zfu", "w03", "yb0", "w02", "yau1", "xa0", "wfu1",
-    "xad1", "yau2", "ybd1", "as", "yad3", "wfd1", "yc0", "xau1", "yau3", "ybu1", "ya4", "xau2", "yaw", "wfu0",
-    "ybu2", "xad2", "wfd0", "ybd2", "wn", "xau3", "ycu1", "x00", "x0u1", "ycu2", "x0d1", "ycd1", "ybd3", "wfar",
-    "pair", "g1", "x100", "ybu3", "x0d2", "ycu3", "yr00", "ycd2", "x10u1", "x10d1", "yb4", "x0u2", "yr0d1", "xad3",
-    "yr0u1", "x10u2", "x10d2", "ycd3", "x0u3", "x0d3", "yr0d2", "yr0u2", "x10u3", "x10d3", "yc4", "ycw", "ybw",
-    "yr0d3", "yr0u3", "xa4", "x04", "x104", "gw", "yr04", "end",
+    "w01", "zg0", "ya0", "yad1", "a0", "zfu", "w00", "yau1", "yad2", "yau2", "yad3", "zfd", "w03", "w02", "xa0",
+    "yb0", "xau1", "yau3", "ybd1", "yc0", "ybu1", "xad1", "wfu0", "xau2", "ya4", "as", "ycu1", "wfd0", "xau3",
+    "ybd2", "ybu2", "wfu1", "xad2", "yaw", "wn", "wfd1", "ycd1", "x00", "wfar0", "ycd2", "xad3", "x0u1", "x0d1",
+    "yr00", "ybu3", "ycd3", "xa4", "wfar1", "g1", "x100", "x0u2", "x0d2", "yr10", "ycu2", "ybd3", "x10u1", "x10d1",
+    "yr0d1", "yr0u1", "ycu3", "yr1u1", "yr1d1", "x10u2", "x10d2", "yr0u2", "x0u3", "yb4", "x0d3", "yr0d2", "yr1d2",
+    "yr1u2", "x10u3", "x10d3", "yc4", "yr0d3", "yr0u3", "yr1d3", "x04", "yr1u3", "x104", "ycw", "ybw", "gw", "yr04",
+    "yr14", "end",
 )
 
 
@@ -32,8 +33,7 @@
 
 
 def kernel(sizes, acts_in, weight_in, grad_in, out, grad_acts, grad_weight,
-           acts, acts_t, acts_hi, acts_lo, cols, grads, tile, part, part_in, y_up, y_dn, gpart, x_up, x_dn, swap, swap_in,
-           send_sem, recv_sem, local_sem):
+           acts, acts_t, acts_hi, acts_lo, cols, grads, tile, part, part_in, y_up, y_dn, early, late, send_sem, recv_sem, local_sem):
     n_tok, n_fin, n_fout = sizes
     n_y, n_x = n_fin // 2, n_fout // 2
     t, i, o = lax.axis_index("tok"), lax.axis_index("fin"), lax.axis_index("fout")
@@ -47,7 +47,9 @@
     z_op = (lax.rem(t + 2, n_tok), i, lax.rem(o + n_x, n_fout))
     rows, w_rows = grad_in.shape[0], weight_in.shape[0]
     piece = w_rows // n_x
-    quarter = w_rows // 4
+    depth, width = acts_in.shape[1], weight_in.shape[1]
+    lanes = width // 2
+    w_half = w_rows // 2
 
     def aligned(start, count):
         return pl.ds(pl.multiple_of(start, 8), count)
@@ -55,7 +57,7 @@
     mine = aligned(i * rows, rows)
     loads = [
         pltpu.make_async_copy(grad_in, grads.at[0, mine], local_sem.at[0]),
-        pltpu.make_async_copy(weight_in, tile.at[t], local_sem.at[1]),
+        pltpu.make_async_copy(weight_in, tile.at[aligned(t * w_rows, w_rows)], local_sem.at[1]),
         pltpu.make_async_copy(acts_in, acts, local_sem.at[2]),
     ]
     for load in loads:
@@ -177,7 +179,7 @@
     before, after, across = [lax.rem(t + d, n_tok) for d in (n_tok - 1, 1, 2)]
 
     def w_part(block, k):
-        return tile.at[block, pl.ds(k * quarter, quarter)]
+        return tile.at[aligned(block * w_rows + k // 2 * w_half, w_half), pl.ds(k % 2 * lanes, lanes)]
 
     def w_first(k):
         other = (k + 2) % 4
@@ -198,30 +200,32 @@
         events[f"wfu{k}"] = functools.partial(w_up, k)
         events[f"wfd{k}"] = functools.partial(w_dn, k)
 
-    def out_add(blocks, add):
-        value = None
-        for block in blocks:
-            span = pl.ds(pl.multiple_of(block * w_rows, 16), w_rows)
-            term = dot3((acts_hi[span], acts_lo[span]), halves(tile[block]), 0, 0)
-            value = term if value is None else value + term
-        for m in range(n_y):
-            for k in range(2):
-                rows_of = value[(2 * m + k) * rows:(2 * m + k + 1) * rows]
-                part[k, m] = part[k, m] + rows_of if add else rows_of
+    def out_term(block, columns):
+        span = pl.ds(pl.multiple_of(block * w_rows, 16), w_rows)
+        return dot3((acts_hi[span], acts_lo[span]), halves(tile[aligned(block * w_rows, w_rows), columns]), 0, 0)
+
+    def out_rows(value, m, k):
+        return value[(2 * m + k) * rows:(2 * m + k + 1) * rows]
 
     @event("wn")
     def _():
         got(*[f"w{way}{k}" for way in "ud" for k in range(4)])
-        out_add((t, before, after), False)
-
-    @event("wfar")
-    def _():
-        got("vu0", "vu1", "vd0", "vd1")
-        out_add((across,), True)
-
-    @event("pair")
-    def _():
-        copy("pair", part.at[1 - c], part_in, core)
+        value = out_term(t, pl.ds(0, width)) + out_term(before, pl.ds(0, width)) + out_term(after, pl.ds(0, width))
+        for j in range(2):
+            for m in range(n_y):
+                for k in range(2):
+                    part[j, k, m] = out_rows(value, m, k)[:, j * lanes:(j + 1) * lanes]
+
+    def out_far(j):
+        got(f"vu{j}", f"vd{j}")
+        value = out_term(across, pl.ds(j * lanes, lanes))
+        for k in range(2):
+            for m in range(n_y):
+                part[j, k, m] = part[j, k, m] + out_rows(value, m, k)
+        copy(f"pair{j}", part.at[j, 1 - c], part_in.at[j], core)
+
+    for j in range(2):
+        events[f"wfar{j}"] = functools.partial(out_far, j)
 
     def scatter(key, dest, slots, m, n, up, dn, ready, done):
         last = n // 2 - 1
@@ -253,38 +257,51 @@
 
     row_parts = (pl.ds(0, rows), pl.ds(0, h), pl.ds(h, h))
 
-    def out_ready():
-        got("pair")
-        part[c] = part[c] + part_in[...]
-
-    def out_done(value):
-        out[...] = value
-
-    scatter("yr0", lambda m, k: part.at[c, m, row_parts[k]], lambda way, s, k: (y_up, y_dn)[way].at[s, row_parts[k]],
-            y, n_y, yu, yd, out_ready, out_done)
-
-    pair = t // 2
+    def out_ready(j):
+        got(f"pair{j}")
+        part[j, c] = part[j, c] + part_in[j]
+
+    def out_done(j, value):
+        out[:, j * lanes:(j + 1) * lanes] = value
+
+    def out_scatter(j):
+        scatter(f"yr{j}", lambda m, k: part.at[j, c, m, row_parts[k]], lambda way, s, k: (y_up, y_dn)[way].at[j, s, row_parts[k]],
+                y, n_y, yu, yd, functools.partial(out_ready, j), functools.partial(out_done, j))
+
+    out_scatter(0)
+    out_scatter(1)
+
+    pair, odd = t // 2, lax.rem(t, 2)
+    unit = depth // 6
+    own_at, other_at = pair * 3 * unit, (1 - pair) * 3 * unit
+    first_at, last_at = other_at + 2 * unit * (1 - odd), other_at + unit * odd
     zlo_parts = (pl.ds(0, 2), pl.ds(0, 1), pl.ds(1, 1))
 
-    def ga_compute(k):
-        which = 1 - pair if k else pair
-        blocks = tile[pl.ds(2 * which, 2)].reshape(2 * w_rows, weight_in.shape[1])
+    def ga_store(buffer, blocks):
         value = dot3(halves(grads[0]), halves(blocks), 1, 1)
         for m in range(n_x):
             for z in range(2):
-                gpart[k, m, z] = value[(z * n_x + m) * rows:(z * n_x + m + 1) * rows]
-
-    def ga_scatter(key, k, ready):
+                buffer[m, z] = value[(z * n_x + m) * rows:(z * n_x + m + 1) * rows]
+
+    def ga_early():
+        ga_store(early[0], jnp.concatenate([tile[aligned(own_at, 3 * unit)], tile[aligned(first_at, unit)]], 0))
+
+    def ga_late():
+        ga_store(late[0], tile[aligned(last_at, 2 * unit)])
+
+    def ga_scatter(key, swapped, buffers, ready):
+        buffer, up_in, dn_in, swap, swap_in = buffers
+
         def done(value):
-            swap[k] = value
-            copy(f"l{k}", swap.at[k, 1 - zl], swap_in.at[k], zlo)
-
-        scatter(key, lambda m, j: gpart.at[k, m, zlo_parts[j]], lambda way, s, j: (x_up, x_dn)[way].at[k, s, zlo_parts[j]],
+            swap[...] = value
+            copy(swapped, swap.at[1 - zl], swap_in, zlo)
+
+        scatter(key, lambda m, j: buffer.at[m, zlo_parts[j]], lambda way, s, j: (up_in, dn_in)[way].at[s, zlo_parts[j]],
                 x, n_x, xu, xd, ready, done)
 
-    ga_scatter("x0", 0, functools.partial(ga_compute, 0))
-    events["g1"] = functools.partial(ga_compute, 1)
-    ga_scatter("x10", 1, lambda: None)
+    ga_scatter("x0", "l0", early, ga_early)
+    events["g1"] = ga_late
+    ga_scatter("x10", "l1", late, lambda: None)
 
     @event("gw")
     def _():
@@ -294,13 +311,17 @@
             total = total + dot3(halves(cols[slot]), halves(grads[slot]), 1, 0)
         grad_weight[...] = total
 
+    def columns(start, count):
+        return pl.ds(pl.multiple_of(start, unit), count)
+
     @event("end")
     def _():
-        got("l0", "l1")
-        value = [swap[k, zl] + swap_in[k] for k in range(2)]
-        width = value[0].shape[1]
-        grad_acts[:, :width] = jnp.where(pair == 0, value[0], value[1])
-        grad_acts[:, width:] = jnp.where(pair == 0, value[1], value[0])
+        got("l0")
+        value = early[3][zl] + early[4][...]
+        grad_acts[:, columns(own_at, 3 * unit)] = value[:, :3 * unit]
+        grad_acts[:, columns(first_at, unit)] = value[:, 3 * unit:]
+        got("l1")
+        grad_acts[:, columns(last_at, 2 * unit)] = late[3][zl] + late[4][...]
 
     for name in ORDER:
         events.pop(name)()
@@ -315,7 +336,12 @@
     toks, depth = acts.shape
     w_rows, width = weight.shape
     rows = grad_out.shape[0]
-    half = depth // 2
+    unit = depth // 6
+
+    def scattered(count):
+        shapes = [(n_x, 2), (n_x // 2, 2), (n_x // 2, 2), (2,), ()]
+        return [pltpu.VMEM((*shape, rows, count), F32) for shape in shapes]
+
     vmem = pl.BlockSpec(memory_space=pltpu.VMEM)
     return pl.pallas_call(
         functools.partial(kernel, sizes),
@@ -333,18 +359,15 @@
             pltpu.VMEM((depth, toks), jnp.bfloat16),
             pltpu.VMEM((n_tok, w_rows, toks), F32),
             pltpu.VMEM((n_tok, toks, width), F32),
-            pltpu.VMEM((n_tok, w_rows, width), F32),
-            pltpu.VMEM((2, n_y, rows, width), F32),
-            pltpu.VMEM((n_y, rows, width), F32),
-            pltpu.VMEM((n_y // 2, rows, width), F32),
-            pltpu.VMEM((n_y // 2, rows, width), F32),
-            pltpu.VMEM((2, n_x, 2, rows, half), F32),
-            pltpu.VMEM((2, n_x // 2, 2, rows, half), F32),
-            pltpu.VMEM((2, n_x // 2, 2, rows, half), F32),
-            pltpu.VMEM((2, 2, rows, half), F32),
-            pltpu.VMEM((2, rows, half), F32),
-            pltpu.SemaphoreType.DMA((112,)),
-            pltpu.SemaphoreType.DMA((112,)),
+            pltpu.VMEM((n_tok * w_rows, width), F32),
+            pltpu.VMEM((2, 2, n_y, rows, width // 2), F32),
+            pltpu.VMEM((2, n_y, rows, width // 2), F32),
+            pltpu.VMEM((2, n_y // 2, rows, width // 2), F32),
+            pltpu.VMEM((2, n_y // 2, rows, width // 2), F32),
+            scattered(4 * unit),
+            scattered(2 * unit),
+            pltpu.SemaphoreType.DMA((128,)),
+            pltpu.SemaphoreType.DMA((128,)),
             pltpu.SemaphoreType.DMA((3,)),
         ],
         compiler_params=pltpu.CompilerParams(collective_id=0, has_side_effects=True, vmem_limit_bytes=54 * 2**20),

time: 106 us -> 105 us (level)
  the two profiles are of different devices: /device:TPU:1 before, /device:TPU:2 now
where the time goes in v3:
time: 105 us
  Pallas kernels  99.4 us (95%)
  local copies, waits for them, and re-layouts  4.99 us (5%)
    pallas_call x1, Pallas kernels, shards(): pl.pallas_call(functools.partial(kernel, sizes), out_shape=(jax.ShapeDtyp...  99.4 us
    unnamed x3, local copies, waits for them, and re-layouts  4.99 us

profile of v3, /device:TPU:2, one launch (start us, length us, event | category | flops | bytes accessed | tf_op | source)
XLA Modules:
  0.0 105.1 jit_solution(13048359661684131972)
XLA Ops:
  0.6 99.4 %shard_map.58 = (f32[32,768]{1,0:T(8,128)}, f32[32,768]{1,0:T(8,128)}, f32[192,768]{1,0:T(8,128)}) custom-call(f32[512,768]{1,0:T(8,128)} %acts_in.1, f32[192,768]{1,0:T(8,128)} %weight_in.1, f32[32,768]{1,0:T(8,128)} %grad_in.1), custom_call_target="tpu_custom_call" | custom-call | tf_op jit(solution)/shard_map/pallas_call | solution.py:346
  100.1 1.5 %copy.9 = f32[32,768]{1,0:T(8,128)} copy(f32[32,768]{1,0:T(8,128)} %get-tuple-element.6) | data formatting | bytes 196608
  101.6 1.5 %copy.10 = f32[32,768]{1,0:T(8,128)} copy(f32[32,768]{1,0:T(8,128)} %get-tuple-element.7) | data formatting | bytes 196608
  103.2 1.9 %copy.11 = f32[192,768]{1,0:T(8,128)} copy(f32[192,768]{1,0:T(8,128)} %get-tuple-element.8) | data formatting | bytes 1179648

commit v4 on v3

--- a/solution.py
+++ b/solution.py
@@ -11,13 +11,13 @@
 F32 = jnp.float32
 
 ORDER = (
-    "w01", "zg0", "ya0", "yad1", "a0", "zfu", "w00", "yau1", "yad2", "yau2", "yad3", "zfd", "w03", "w02", "xa0",
-    "yb0", "xau1", "yau3", "ybd1", "yc0", "ybu1", "xad1", "wfu0", "xau2", "ya4", "as", "ycu1", "wfd0", "xau3",
-    "ybd2", "ybu2", "wfu1", "xad2", "yaw", "wn", "wfd1", "ycd1", "x00", "wfar0", "ycd2", "xad3", "x0u1", "x0d1",
-    "yr00", "ybu3", "ycd3", "xa4", "wfar1", "g1", "x100", "x0u2", "x0d2", "yr10", "ycu2", "ybd3", "x10u1", "x10d1",
-    "yr0d1", "yr0u1", "ycu3", "yr1u1", "yr1d1", "x10u2", "x10d2", "yr0u2", "x0u3", "yb4", "x0d3", "yr0d2", "yr1d2",
-    "yr1u2", "x10u3", "x10d3", "yc4", "yr0d3", "yr0u3", "yr1d3", "x04", "yr1u3", "x104", "ycw", "ybw", "gw", "yr04",
-    "yr14", "end",
+    "zg0", "ya0", "a0", "yad1", "yau1", "w03", "yad2", "w01", "zfd", "yau2", "w00", "yad3", "zfu", "xa0", "yb0",
+    "yau3", "xad1", "as", "ybu1", "ya4", "yc0", "xau1", "ybd1", "w02", "xad2", "ycu1", "wfu0", "ycd1", "yaw",
+    "xau2", "ybd2", "ybu2", "xad3", "wfu1", "wfd0", "ycu2", "wn", "wfd1", "xau3", "x00", "ycu3", "ycd2", "wfar0",
+    "gwa", "ybd3", "x0u1", "x0d1", "yr00", "ycd3", "wfar1", "g1", "x100", "x0u2", "x0d2", "yr0u1", "yr10", "yr0d1",
+    "x10u1", "x10d1", "ybu3", "yc4", "yr1u1", "yr1d1", "yr0u2", "x10u2", "x10d2", "yr0d2", "x0u3", "x0d3", "yr1d2",
+    "yr1u2", "yb4", "x10u3", "x10d3", "yr0u3", "yr0d3", "yr1d3", "x04", "yr1u3", "xa4", "x104", "ybw", "gwb", "ycw",
+    "gwc", "yr04", "yr14", "end",
 )
 
 
@@ -303,13 +303,19 @@
     events["g1"] = ga_late
     ga_scatter("x10", "l1", late, lambda: None)
 
-    @event("gw")
+    @event("gwa")
     def _():
         own = pl.ds(pl.multiple_of(t * w_rows, 16), w_rows)
-        total = dot3((acts_hi[own], acts_lo[own]), halves(grads[0]), 1, 0)
-        for slot in range(1, n_tok):
+        grad_weight[...] = dot3((acts_hi[own], acts_lo[own]), halves(grads[0]), 1, 0)
+
+    def gw_add(*slots):
+        total = grad_weight[...]
+        for slot in slots:
             total = total + dot3(halves(cols[slot]), halves(grads[slot]), 1, 0)
         grad_weight[...] = total
+
+    events["gwb"] = functools.partial(gw_add, 1, 2)
+    events["gwc"] = functools.partial(gw_add, 3)
 
     def columns(start, count):
         return pl.ds(pl.multiple_of(start, unit), count)

time: 105 us -> 108 us (1.029)
  the two profiles are of different devices: /device:TPU:2 before, /device:TPU:50 now
where the time goes in v4:
time: 108 us; the launch traced here: 107 us
  Pallas kernels  102 us (94%)
  local copies, waits for them, and re-layouts  4.99 us (5%)
    pallas_call x1, Pallas kernels, shards(): pl.pallas_call(functools.partial(kernel, sizes), out_shape=(jax.ShapeDtyp...  102 us
    unnamed x3, local copies, waits for them, and re-layouts  4.99 us

profile of v4, /device:TPU:50, one launch (start us, length us, event | category | flops | bytes accessed | tf_op | source)
XLA Modules:
  0.0 107.4 jit_solution(17713279112987160330)
XLA Ops:
  0.6 101.8 %shard_map.58 = (f32[32,768]{1,0:T(8,128)}, f32[32,768]{1,0:T(8,128)}, f32[192,768]{1,0:T(8,128)}) custom-call(f32[512,768]{1,0:T(8,128)} %acts_in.1, f32[192,768]{1,0:T(8,128)} %weight_in.1, f32[32,768]{1,0:T(8,128)} %grad_in.1), custom_call_target="tpu_custom_call" | custom-call | tf_op jit(solution)/shard_map/pallas_call | solution.py:352
  102.4 1.5 %copy.9 = f32[32,768]{1,0:T(8,128)} copy(f32[32,768]{1,0:T(8,128)} %get-tuple-element.6) | data formatting | bytes 196608
  104.0 1.5 %copy.10 = f32[32,768]{1,0:T(8,128)} copy(f32[32,768]{1,0:T(8,128)} %get-tuple-element.7) | data formatting | bytes 196608
  105.5 1.9 %copy.11 = f32[192,768]{1,0:T(8,128)} copy(f32[192,768]{1,0:T(8,128)} %get-tuple-element.8) | data formatting | bytes 1179648

commit v5 on v3

--- a/solution.py
+++ b/solution.py
@@ -11,13 +11,13 @@
 F32 = jnp.float32
 
 ORDER = (
-    "w01", "zg0", "ya0", "yad1", "a0", "zfu", "w00", "yau1", "yad2", "yau2", "yad3", "zfd", "w03", "w02", "xa0",
-    "yb0", "xau1", "yau3", "ybd1", "yc0", "ybu1", "xad1", "wfu0", "xau2", "ya4", "as", "ycu1", "wfd0", "xau3",
-    "ybd2", "ybu2", "wfu1", "xad2", "yaw", "wn", "wfd1", "ycd1", "x00", "wfar0", "ycd2", "xad3", "x0u1", "x0d1",
-    "yr00", "ybu3", "ycd3", "xa4", "wfar1", "g1", "x100", "x0u2", "x0d2", "yr10", "ycu2", "ybd3", "x10u1", "x10d1",
-    "yr0d1", "yr0u1", "ycu3", "yr1u1", "yr1d1", "x10u2", "x10d2", "yr0u2", "x0u3", "yb4", "x0d3", "yr0d2", "yr1d2",
-    "yr1u2", "x10u3", "x10d3", "yc4", "yr0d3", "yr0u3", "yr1d3", "x04", "yr1u3", "x104", "ycw", "ybw", "gw", "yr04",
-    "yr14", "end",
+    "zg0", "ya0", "w01", "a0", "zfu", "w00", "zfd", "yad1", "yau1", "yb0", "w03", "xa0", "w02", "xau1", "xad1",
+    "yau2", "yad2", "ybu1", "xau2", "yad3", "xad2", "yau3", "wfu0", "yc0", "wfd0", "xad3", "as", "ya4", "ycd1",
+    "wfd1", "ycu1", "ybu2", "wfu1", "ybd1", "wn", "xau3", "yaw", "x00", "ycu2", "ybd2", "ycd2", "x0u1", "xa4",
+    "ybu3", "ycu3", "x0d1", "wfar0", "wfar1", "g1", "x100", "x0u2", "yr00", "yr10", "ybd3", "x10d1", "x10u1",
+    "x0d2", "yr0u1", "ycd3", "yr1d1", "yr1u1", "yr0d1", "x10u2", "x10d2", "yr0u2", "x0u3", "x0d3", "yr1u2", "yr0d2",
+    "yr1d2", "x10u3", "x10d3", "yb4", "yc4", "yr0u3", "yr1u3", "yr0d3", "x04", "ybw", "yr1d3", "ycw", "x104", "gw",
+    "yr14", "yr04", "end",
 )
 
 

time: 105 us -> 105 us (level)
  the two profiles are of different devices: /device:TPU:2 before, /device:TPU:1 now
where the time goes in v5:
time: 105 us; the launch traced here: 103 us
  Pallas kernels  97.7 us (93%)
  local copies, waits for them, and re-layouts  4.99 us (5%)
    pallas_call x1, Pallas kernels, shards(): pl.pallas_call(functools.partial(kernel, sizes), out_shape=(jax.ShapeDtyp...  97.7 us
    unnamed x3, local copies, waits for them, and re-layouts  4.99 us

profile of v5, /device:TPU:1, one launch (start us, length us, event | category | flops | bytes accessed | tf_op | source)
XLA Modules:
  0.0 103.3 jit_solution(7479311534219062471)
XLA Ops:
  0.6 97.7 %shard_map.58 = (f32[32,768]{1,0:T(8,128)}, f32[32,768]{1,0:T(8,128)}, f32[192,768]{1,0:T(8,128)}) custom-call(f32[512,768]{1,0:T(8,128)} %acts_in.1, f32[192,768]{1,0:T(8,128)} %weight_in.1, f32[32,768]{1,0:T(8,128)} %grad_in.1), custom_call_target="tpu_custom_call" | custom-call | tf_op jit(solution)/shard_map/pallas_call | solution.py:346
  98.4 1.5 %copy.9 = f32[32,768]{1,0:T(8,128)} copy(f32[32,768]{1,0:T(8,128)} %get-tuple-element.6) | data formatting | bytes 196608
  99.9 1.5 %copy.10 = f32[32,768]{1,0:T(8,128)} copy(f32[32,768]{1,0:T(8,128)} %get-tuple-element.7) | data formatting | bytes 196608
  101.4 1.9 %copy.11 = f32[192,768]{1,0:T(8,128)} copy(f32[192,768]{1,0:T(8,128)} %get-tuple-element.8) | data formatting | bytes 1179648
